TPU v7x, 32 devices: a whole 2x2x4 slice. The times are simulated.
32 devices in a mesh: dp: 4 (over y, x), expert: 8 (over z, core).
Axes of the slice: x: 2, y: 2, z: 4, core: 2. Of those that a mesh axis runs over, the one named last changes fastest.
Arguments:
- tokens: bfloat16 [4096, 1024], P(('dp', 'expert')), may hold values from -6 to 6
- expert_ids: int32 [4096, 6], P(('dp', 'expert')), may hold values from 0 to 15, all different within a row; in each aligned block of 128 rows (0 to 127, 128 to 255, ...) at most 49 rows name the same one
- router_gates: float32 [4096, 6], P(('dp', 'expert')), may hold values from 0.05 to 1
- w_in: bfloat16 [16, 2, 704, 1024], P('expert', None, 'dp'), may hold values from -0.1875 to 0.1875
- w_down: bfloat16 [16, 704, 1024], P('expert', 'dp'), may hold values from -0.21875 to 0.21875
- cotangent: bfloat16 [4096, 1024], P(('dp', 'expert')), may hold values from -6 to 6
Outputs:
- layer_output: bfloat16 [4096, 1024], P(('dp', 'expert'))
- token_grads: bfloat16 [4096, 1024], P(('dp', 'expert'))
- gate_grads: float32 [4096, 6], P(('dp', 'expert'))
Inputs may be any that keep to these rules, and one draw needn't show every extreme that they name: `expert_ids`: each row names 6 different experts. The rows of one device name no expert more than 49 times, and in every draw some device names some expert exactly 49 times.
All inputs are finite; a program needn't handle non-finite values.
Results may differ from a plain program's by a relative error of at most 0.0064.
Values may be sent and summed in bfloat16 or wider, within the bound.
A program may use at most 64 MiB of HBM per device.

v0:
```python
import jax
import jax.numpy as jnp
from jax import lax
from jax.sharding import PartitionSpec as P


def expert_terms(x, cot, ids, gates, full_in, full_down, first_expert):
    exp_local, _, hidden_width, _ = full_in.shape
    out_sum = jnp.zeros(x.shape, jnp.float32)
    grad_sum = jnp.zeros(x.shape, jnp.float32)
    gate_sum = jnp.zeros(gates.shape, jnp.float32)
    nt = (((1,), (1,)), ((), ()))
    nn = (((1,), (0,)), ((), ()))

    def dot(a, b, dims):
        return lax.dot_general(a, b, dims, preferred_element_type=jnp.float32)

    for e in range(exp_local):
        chosen = ids == first_expert + e
        g = jnp.sum(jnp.where(chosen, gates, 0.0), axis=1, keepdims=True)
        w_pair = full_in[e].reshape(2 * hidden_width, -1)
        both = dot(x, w_pair, nt)
        gate_pre, up_pre = both[:, :hidden_width], both[:, hidden_width:]
        s = jax.nn.sigmoid(gate_pre)
        act = gate_pre * s
        hidden = act * up_pre
        gh = dot(cot, full_down[e], nt)
        gate_sum += jnp.where(chosen, jnp.sum(hidden * gh, axis=1, keepdims=True), 0.0)
        out_sum += dot((hidden * g).astype(jnp.bfloat16), full_down[e], nn)
        gh = gh * g
        grad_up = (gh * act).astype(jnp.bfloat16)
        grad_gate = (gh * up_pre * s * (1.0 + gate_pre * (1.0 - s))).astype(jnp.bfloat16)
        grad_sum += dot(jnp.concatenate([grad_gate, grad_up], axis=1), w_pair, nn)
    return out_sum.astype(jnp.bfloat16), grad_sum.astype(jnp.bfloat16), gate_sum


def body(tokens, expert_ids, router_gates, w_in, w_down, cotangent):
    exp_local = w_in.shape[0]
    first_expert = lax.axis_index("expert") * exp_local
    x = lax.all_gather(tokens, "expert", axis=0, tiled=True)
    cot = lax.all_gather(cotangent, "expert", axis=0, tiled=True)
    ids = lax.all_gather(expert_ids, "expert", axis=0, tiled=True)
    gates = lax.all_gather(router_gates, "expert", axis=0, tiled=True)
    full_in = lax.all_gather(w_in, "dp", axis=2, tiled=True)
    full_down = lax.all_gather(w_down, "dp", axis=1, tiled=True)
    rows = x.shape[0]
    if rows <= 1024:
        out, grad, gate = expert_terms(x, cot, ids, gates, full_in, full_down, first_expert)
    else:
        parts = rows // 512
        out, grad, gate = lax.map(
            lambda a: expert_terms(*a, full_in, full_down, first_expert),
            tuple(v.reshape(parts, 512, v.shape[1]) for v in (x, cot, ids, gates)),
        )
        out, grad, gate = (v.reshape(rows, v.shape[2]) for v in (out, grad, gate))
    return tuple(
        lax.psum_scatter(v, "expert", scatter_dimension=0, tiled=True) for v in (out, grad, gate)
    )


def solution(mesh):
    rows = P(("dp", "expert"), None)
    placed = (rows, rows, rows, P("expert", None, "dp", None), P("expert", "dp", None), rows)
    return jax.shard_map(
        body, mesh=mesh, in_specs=placed, out_specs=(rows, rows, rows), check_vma=False
    )
```

profile of v0, /device:TPU:10, one launch (start us, length us, event | category | flops | bytes accessed | tf_op | source)
XLA Modules:
  0.0 300.5 jit_solution(7391338193481564161)
XLA Ops:
  7.2 0.7 all-gather.7.cloned.1.call-update
  7.9 0.7 all-gather.5.cloned.1.call-update
  8.7 0.7 all-gather.11.cloned.1.call-update
  9.4 0.5 all-gather.9.cloned.1.call-update
  10.0 14.3 %all_gather.20 = s32[1024,6]{0,1:T(8,128)S(1)} all-gather(s32[128,6]{0,1:T(8,128)} %param.7), channel_id=1, replica_groups=mesh['dp'=4,'expert'=8] {'expert'}, dimensions={0}, use_global_device_ids=true | all-gather | bytes 27648 | tf_op jit(solution)/shard_map/all_gather | solution.py:42
  24.3 14.1 %all_gather.21 = f32[1024,6]{0,1:T(8,128)S(1)} all-gather(f32[128,6]{0,1:T(8,128)} %param.8), channel_id=1, replica_groups=mesh['dp'=4,'expert'=8] {'expert'}, dimensions={0}, use_global_device_ids=true | all-gather | bytes 27648 | tf_op jit(solution)/shard_map/all_gather | solution.py:43
  38.5 38.4 %all-gather.7.cloned.1.call-done = bf16[2,2,704,1024]{3,2,1,0:T(8,128)(2,1)} async-done(((bf16[2,2,176,1024]{3,2,1,0:T(8,128)(2,1)}), bf16[2,2,704,1024]{3,2,1,0:T(8,128)(2,1)}) %all-gather.7.cloned.1.call-update) | async-done | bytes 5767184 | tf_op jit(solution)/shard_map/all_gather | solution.py:44
  76.8 5.2 %fusion.21 = (bf16[1,2,704,1024]{3,2,1,0:T(8,128)(2,1)}, bf16[1,2,704,1024]{3,2,1,0:T(8,128)(2,1)S(1)}) fusion(bf16[2,2,704,1024]{3,2,1,0:T(8,128)(2,1)} %all-gather.7.cloned.1.call-done), kind=kLoop, calls=%fused_computation.38 | loop fusion | bytes 11534336 | tf_op jit(solution)/shard_map/slice | solution.py:21
  82.0 25.5 %all-gather.5.cloned.1.call-done = bf16[1024,1024]{1,0:T(8,128)(2,1)} async-done(((bf16[128,1024]{1,0:T(8,128)(2,1)}), bf16[1024,1024]{1,0:T(8,128)(2,1)}) %all-gather.5.cloned.1.call-update) | async-done | bytes 2097168 | tf_op jit(solution)/shard_map/all_gather | solution.py:40
  107.5 7.0 %fusion.23 = f32[1024,1408]{1,0:T(8,128)} fusion(bf16[1024,1024]{1,0:T(8,128)(2,1)} %all-gather.5.cloned.1.call-done, bf16[1408,1024]{1,0:T(8,128)(2,1)S(1)} %bitcast.24), kind=kOutput, calls=%fused_computation.40 | convolution fusion | flops 2952790016 | bytes 10747904 | tf_op jit(solution)/shard_map/dot_general | solution.py:16
  114.5 5.3 %fusion.22 = f32[1024,1408]{1,0:T(8,128)} fusion(bf16[1024,1024]{1,0:T(8,128)(2,1)S(1)} %copy-done.8, bf16[1408,1024]{1,0:T(8,128)(2,1)S(1)} %bitcast.26), kind=kOutput, calls=%fused_computation.39 | convolution fusion | flops 2952790016 | bytes 10747904 | tf_op jit(solution)/shard_map/dot_general | solution.py:16
  119.8 17.9 %all-gather.11.cloned.1.call-done = bf16[1024,1024]{1,0:T(8,128)(2,1)} async-done(((bf16[128,1024]{1,0:T(8,128)(2,1)}), bf16[1024,1024]{1,0:T(8,128)(2,1)}) %all-gather.11.cloned.1.call-update) | async-done | bytes 2097168 | tf_op jit(solution)/shard_map/all_gather | solution.py:41
  137.8 43.0 %all-gather.9.cloned.1.call-done = bf16[2,704,1024]{2,1,0:T(8,128)(2,1)} async-done(((bf16[2,176,1024]{2,1,0:T(8,128)(2,1)}), bf16[2,704,1024]{2,1,0:T(8,128)(2,1)}) %all-gather.9.cloned.1.call-update) | async-done | bytes 2883600 | tf_op jit(solution)/shard_map/all_gather | solution.py:45
  180.8 7.7 %multiply_reduce_fusion = (f32[1024]{0:T(1024)S(1)}, f32[1024,704]{1,0:T(8,128)}) fusion(f32[1024,1408]{1,0:T(8,128)} %fusion.23, bf16[1024,1024]{1,0:T(8,128)(2,1)} %all-gather.11.cloned.1.call-done, bf16[2,704,1024]{2,1,0:T(8,128)(2,1)} %all-gather.9.cloned.1.call-done), kind=kOutput, calls=%fused_computation.2 | convolution fusion | flops 1481440256 | bytes 12718080 | tf_op jit(solution)/shard_map/dot_general | solution.py:16
  188.5 3.6 %multiply_reduce_fusion.1 = (f32[1024]{0:T(1024)S(1)}, f32[1024,704]{1,0:T(8,128)}) fusion(f32[1024,1408]{1,0:T(8,128)S(1)} %copy-done, bf16[1024,1024]{1,0:T(8,128)(2,1)S(1)} %copy-done.7, bf16[2,704,1024]{2,1,0:T(8,128)(2,1)S(1)} %copy-done.5), kind=kOutput, calls=%fused_computation.3 | convolution fusion | flops 1481440256 | bytes 12718080 | tf_op jit(solution)/shard_map/dot_general | solution.py:16
  192.1 0.6 select_add_fusion
  192.8 5.4 %fusion.12 = f32[1024,1024]{1,0:T(8,128)S(1)} fusion(f32[1024]{0:T(1024)S(1)} %get-tuple-element.4, bf16[2,704,1024]{2,1,0:T(8,128)(2,1)} %all-gather.9.cloned.1.call-done, f32[1024,1408]{1,0:T(8,128)} %fusion.22), kind=kOutput, calls=%fused_computation.24 | convolution fusion | flops 1481441280 | bytes 11931648 | tf_op jit(solution)/shard_map/dot_general | solution.py:16
  198.3 3.6 %add_convert_fusion.1 = bf16[1024,1024]{1,0:T(8,128)(2,1)} fusion(f32[1024,1024]{1,0:T(8,128)S(1)} %fusion.12, f32[1024]{0:T(1024)S(1)} %get-tuple-element.3, bf16[2,704,1024]{2,1,0:T(8,128)(2,1)S(1)} %copy-done.6, f32[1024,1408]{1,0:T(8,128)S(1)} %bitcast.23), kind=kOutput, calls=%fused_computation.1 | convolution fusion | flops 1483538432 | bytes 14028800 | tf_op jit(solution)/shard_map/dot_general | solution.py:16
  202.1 8.5 %multiply_convert_fusion.1 = (bf16[1024,704]{1,0:T(8,128)(2,1)S(1)}, bf16[1024,704]{1,0:T(8,128)(2,1)S(1)}, bf16[1024,704]{1,0:T(8,128)(2,1)S(1)}, bf16[1024,704]{1,0:T(8,128)(2,1)S(1)}) fusion(f32[1024,1408]{1,0:T(8,128)} %fusion.23, f32[1024,704]{1,0:T(8,128)} %get-tuple-element.15, f32[1024]{0:T(1024)S(1)} %get-tuple-element.3, f32[1024,1408]{1,0:T(8,128)} %fusion.22, ...), kind=kLoop, calls=%fused_computation.5 | loop fusion | flops 20185088 | bytes 23076864 | tf_op jit(solution)/shard_map/convert_element_type | solution.py:32
  210.7 3.4 %fusion.2 = f32[1024,1024]{1,0:T(8,128)S(1)} fusion(bf16[1408,1024]{1,0:T(8,128)(2,1)S(1)} %bitcast.27, bf16[1024,704]{1,0:T(8,128)(2,1)S(1)} %get-tuple-element.18, bf16[1024,704]{1,0:T(8,128)(2,1)S(1)} %get-tuple-element.19), kind=kOutput, calls=%fused_computation.16 | convolution fusion | flops 2958557184 | bytes 9961472 | tf_op jit(solution)/shard_map/dot_general | solution.py:16
  214.1 4.8 %add_convert_fusion = bf16[1024,1024]{1,0:T(8,128)(2,1)} fusion(f32[1024,1024]{1,0:T(8,128)S(1)} %fusion.2, bf16[1408,1024]{1,0:T(8,128)(2,1)S(1)} %bitcast.25, bf16[1024,704]{1,0:T(8,128)(2,1)S(1)} %get-tuple-element.9, bf16[1024,704]{1,0:T(8,128)(2,1)S(1)} %get-tuple-element.8), kind=kOutput, calls=%fused_computation | convolution fusion | flops 2960654336 | bytes 12058624 | tf_op jit(solution)/shard_map/dot_general | solution.py:16
  219.0 0.4 reduce-scatter.8.cloned.1.call-done
  219.4 36.6 %reduce-scatter.4.cloned.1.call-done = bf16[128,1024]{1,0:T(8,128)(2,1)} async-done(((bf16[1024,1024]{1,0:T(8,128)(2,1)}), bf16[128,1024]{1,0:T(8,128)(2,1)}) %reduce-scatter.4.cloned.1.call-update) | async-done | bytes 262160 | tf_op jit(solution)/shard_map/reduce_scatter | solution.py:57
  256.0 37.6 %reduce-scatter.6.cloned.1.call-done = bf16[128,1024]{1,0:T(8,128)(2,1)} async-done(((bf16[1024,1024]{1,0:T(8,128)(2,1)}), bf16[128,1024]{1,0:T(8,128)(2,1)}) %reduce-scatter.6.cloned.1.call-update) | async-done | bytes 262160 | tf_op jit(solution)/shard_map/reduce_scatter | solution.py:57
  (34 shorter events, 0.6 us)
Async XLA Ops:
  7.2 69.6 %all-gather.7.cloned.1.call-start = ((), (), s32[]{:S(2)}) async-start(), calls=%async_computation.4 | async-start | bytes 7208960 | tf_op jit(solution)/shard_map/all_gather | solution.py:44
  7.9 99.6 %all-gather.5.cloned.1.call-start = ((), (), s32[]{:S(2)}) async-start(), calls=%async_computation.3 | async-start | bytes 2359296 | tf_op jit(solution)/shard_map/all_gather | solution.py:40
  8.6 129.1 %all-gather.11.cloned.1.call-start = ((), (), s32[]{:S(2)}) async-start(), calls=%async_computation.7 | async-start | bytes 2359296 | tf_op jit(solution)/shard_map/all_gather | solution.py:41
  9.4 171.4 %all-gather.9.cloned.1.call-start = ((), (), s32[]{:S(2)}) async-start(), calls=%async_computation.5 | async-start | bytes 3604480 | tf_op jit(solution)/shard_map/all_gather | solution.py:45
  10.0 209.4 %reduce-scatter.8.cloned.1.call-start = ((), (), s32[]{:S(2)}) async-start(), calls=%async_computation.9 | async-start | bytes 36864 | tf_op jit(solution)/shard_map/reduce_scatter | solution.py:57
  82.0 32.5 %copy-start.1 = (bf16[1,2,704,1024]{3,2,1,0:T(8,128)(2,1)}, bf16[1,2,704,1024]{3,2,1,0:T(8,128)(2,1)S(1)}, u32[]{:S(2)}) copy-start(bf16[1,2,704,1024]{3,2,1,0:T(8,128)(2,1)S(1)} %get-tuple-element.13) | copy-start | bytes 8650756
  107.5 7.0 %copy-start.3 = (bf16[1,2,704,1024]{3,2,1,0:T(8,128)(2,1)S(1)}, bf16[1,2,704,1024]{3,2,1,0:T(8,128)(2,1)}, u32[]{:S(2)}) copy-start(bf16[1,2,704,1024]{3,2,1,0:T(8,128)(2,1)} %get-tuple-element.12) | copy-start | bytes 8650756
  107.5 7.0 %copy-start.8 = (bf16[1024,1024]{1,0:T(8,128)(2,1)S(1)}, bf16[1024,1024]{1,0:T(8,128)(2,1)}, u32[]{:S(2)}) copy-start(bf16[1024,1024]{1,0:T(8,128)(2,1)} %all-gather.5.cloned.1.call-done) | copy-start | bytes 6291460
  180.8 7.7 %copy-start = (f32[1024,1408]{1,0:T(8,128)S(1)}, f32[1024,1408]{1,0:T(8,128)}, u32[]{:S(2)}) copy-start(f32[1024,1408]{1,0:T(8,128)} %fusion.22) | copy-start | bytes 17301508
  180.8 7.7 %copy-start.5 = (bf16[2,704,1024]{2,1,0:T(8,128)(2,1)S(1)}, bf16[2,704,1024]{2,1,0:T(8,128)(2,1)}, u32[]{:S(2)}) copy-start(bf16[2,704,1024]{2,1,0:T(8,128)(2,1)} %all-gather.9.cloned.1.call-done) | copy-start | bytes 8650756
  180.8 7.7 %copy-start.7 = (bf16[1024,1024]{1,0:T(8,128)(2,1)S(1)}, bf16[1024,1024]{1,0:T(8,128)(2,1)}, u32[]{:S(2)}) copy-start(bf16[1024,1024]{1,0:T(8,128)(2,1)} %all-gather.11.cloned.1.call-done) | copy-start | bytes 6291460
  188.5 9.7 %slice-start = ((s8[5767168]{0:T(1024)(128)(4,1)}), s8[1572864]{0:T(1024)(128)(4,1)S(1)}, s32[]{:S(2)}) async-start(s8[5767168]{0:T(1024)(128)(4,1)} %bitcast.22), calls=%async_computation.10 | async-start | bytes 3145728
  192.7 63.3 %reduce-scatter.4.cloned.1.call-start = ((), (), s32[]{:S(2)}) async-start(), calls=%async_computation.6 | async-start | bytes 2359296 | tf_op jit(solution)/shard_map/reduce_scatter | solution.py:57
  192.8 5.4 %slice-start.1 = ((s8[5767168]{0:T(1024)(128)(4,1)}), s8[4194304]{0:T(1024)(128)(4,1)S(1)}, s32[]{:S(2)}) async-start(s8[5767168]{0:T(1024)(128)(4,1)} %bitcast.22), calls=%async_computation.11 | async-start | bytes 8388608
  192.8 5.4 %copy-start.6 = (bf16[2,704,1024]{2,1,0:T(8,128)(2,1)S(1)}, bf16[2,704,1024]{2,1,0:T(8,128)(2,1)}, u32[]{:S(2)}) copy-start(bf16[2,704,1024]{2,1,0:T(8,128)(2,1)} %all-gather.9.cloned.1.call-done) | copy-start | bytes 8650756
  201.9 91.7 %reduce-scatter.6.cloned.1.call-start = ((), (), s32[]{:S(2)}) async-start(), calls=%async_computation.8 | async-start | bytes 2359296 | tf_op jit(solution)/shard_map/reduce_scatter | solution.py:57
  202.1 8.5 %copy-start.4 = (bf16[1,2,704,1024]{3,2,1,0:T(8,128)(2,1)S(1)}, bf16[1,2,704,1024]{3,2,1,0:T(8,128)(2,1)}, u32[]{:S(2)}) copy-start(bf16[1,2,704,1024]{3,2,1,0:T(8,128)(2,1)} %get-tuple-element.12) | copy-start | bytes 8650756
  210.7 3.4 %copy-start.2 = (bf16[1,2,704,1024]{3,2,1,0:T(8,128)(2,1)S(1)}, bf16[1,2,704,1024]{3,2,1,0:T(8,128)(2,1)}, u32[]{:S(2)}) copy-start(bf16[1,2,704,1024]{3,2,1,0:T(8,128)(2,1)} %copy-done.1) | copy-start | bytes 8650756
Sparse Core Ops, SparseCore 0:
  9.8 66.9 all-gather.6
  78.4 29.0 all-gather.4
  109.1 28.5 all-gather.10
  139.5 41.3 all-gather.8
  192.8 26.4 reduce-scatter.7
  222.2 33.7 reduce-scatter.3
  259.0 34.6 reduce-scatter.5
where the time goes:
time: 306 us; the launch traced here: 300 us
  waiting for transfers between devices  202 us (66%)
  matrix products  40.8 us (13%)
  blocking collectives  28.4 us (9%)
  between operations  14.3 us (5%)
  other arithmetic  9.17 us (3%)
  local copies, waits for them, and re-layouts  5.23 us (2%)
    reduce_scatter x3, waiting for transfers between devices, body(): lax.psum_scatter(v, 'expert', scatter_dimension=0, tiled=True)  74.7 us
    all_gather x1, waiting for transfers between devices, body(): full_down = lax.all_gather(w_down, 'dp', axis=1, tiled=True)  43 us
    dot_general x8, matrix products, dot(): return lax.dot_general(a, b, dims, preferred_element_type=jnp.float32)  40.8 us
    all_gather x1, waiting for transfers between devices, body(): full_in = lax.all_gather(w_in, 'dp', axis=2, tiled=True)  38.4 us
    all_gather x1, waiting for transfers between devices, body(): x = lax.all_gather(tokens, 'expert', axis=0, tiled=True)  25.5 us
    all_gather x1, waiting for transfers between devices, body(): cot = lax.all_gather(cotangent, 'expert', axis=0, tiled=True)  17.9 us
    all_gather x1, blocking collectives, body(): ids = lax.all_gather(expert_ids, 'expert', axis=0, tiled=True)  14.3 us
    all_gather x1, blocking collectives, body(): gates = lax.all_gather(router_gates, 'expert', axis=0, tiled=True)  14.1 us
  transfers between devices with their start and end apart: 7, of which 7 were waited for; matrix products, arithmetic and copies ran while one was open for 14% of the time, Pallas kernels for 0%

commit v1 on v0

--- a/solution.py
+++ b/solution.py
@@ -1,7 +1,11 @@
 import jax
 import jax.numpy as jnp
 from jax import lax
+from jax.experimental import pallas as pl
+from jax.experimental.pallas import tpu as pltpu
 from jax.sharding import PartitionSpec as P
+
+MESH = pl.DeviceIdType.MESH
 
 
 def expert_terms(x, cot, ids, gates, full_in, full_down, first_expert):
@@ -58,9 +62,390 @@
     )
 
 
+def fused_kernel(
+    tok_in, cot_in, gm_in, win_in, wd_in,
+    out_ref, grad_ref, gv_ref,
+    tok, cot, gm, win, wd, acc, gacc, sibs, sibr, gsibs, gsibr, snd, gsnd, up, dn, gup, gdn,
+    load_sem, ag_ss, ag_rs, sg_ss, sg_rs, w_ss, w_rs, f_ss, f_rs, sb_ss, sb_rs, ch_ss, up_rs, dn_rs,
+):
+    dp, ex = lax.axis_index("dp"), lax.axis_index("expert")
+    y, x = dp // 2, dp % 2
+    z, c = ex // 2, ex % 2
+    dp_x, dp_y = y * 2 + (1 - x), (1 - y) * 2 + x
+    sibling = (dp, z * 2 + 1 - c)
+    above, below = (dp, ex + 2), (dp, ex - 2)
+    x_peer, y_peer = (dp_x, ex), (dp_y, ex)
+    levels = tok.shape[0] // 2
+    top = levels - 1
+    part = win_in.shape[2]
+    rows, width = tok_in.shape
+    cut = part // 32 * 16 + 16
+    has_above, has_below = z < top, z > 0
+
+    barrier = pltpu.get_barrier_semaphore()
+    for peer in (sibling, x_peer, y_peer):
+        pl.semaphore_signal(barrier, inc=1, device_id=peer, device_id_type=MESH)
+
+    @pl.when(has_above)
+    def _():
+        pl.semaphore_signal(barrier, inc=1, device_id=above, device_id_type=MESH)
+
+    @pl.when(has_below)
+    def _():
+        pl.semaphore_signal(barrier, inc=1, device_id=below, device_id_type=MESH)
+
+    pl.semaphore_wait(barrier, 3 + jnp.where(has_above, 1, 0) + jnp.where(has_below, 1, 0))
+
+    def remote(src, dst, ss, rs, peer):
+        return pltpu.make_async_remote_copy(
+            src_ref=src, dst_ref=dst, send_sem=ss, recv_sem=rs, device_id=peer, device_id_type=MESH
+        )
+
+    def unit_rows(s):
+        return pl.ds(pl.multiple_of(s * part, 16), part)
+
+    def weights_direct(e, axis):
+        peer = (x_peer, y_peer)[axis]
+        mine = unit_rows(dp)
+        return [
+            remote(win_in.at[e], win.at[e, :, mine], w_ss.at[e, axis, 0], w_rs.at[e, axis, 0], peer),
+            remote(wd_in.at[e], wd.at[e, mine], w_ss.at[e, axis, 1], w_rs.at[e, axis, 1], peer),
+        ]
+
+    def weights_forward(e, axis):
+        peer = (x_peer, y_peer)[axis]
+        s = (dp_y, dp_x)[axis]
+        base = pl.multiple_of(s * part, 16)
+        mats = win.at[e, axis, unit_rows(s)]
+        down = wd.at[e, pl.ds(base, cut)] if axis == 0 else wd.at[e, pl.ds(base + cut, part - cut)]
+        return [
+            remote(mats, mats, f_ss.at[e, axis, 0], f_rs.at[e, axis, 0], peer),
+            remote(down, down, f_ss.at[e, axis, 1], f_rs.at[e, axis, 1], peer),
+        ]
+
+    def token_hop(step, direction, own):
+        src = ex + 2 * step if direction else ex - 2 * step
+        peer = below if direction else above
+        refs = (tok, cot, gm)
+        srcs = (tok_in, cot_in, gm_in) if own else [r.at[src] for r in refs]
+        return [
+            remote(a, r.at[src], ag_ss.at[direction, step, i], ag_rs.at[direction, step, i], peer)
+            for i, (a, r) in enumerate(zip(srcs, refs))
+        ]
+
+    def token_sibling(level, own=False):
+        refs = (tok, cot, gm)
+        src = level * 2 + c
+        srcs = (tok_in, cot_in, gm_in) if own else [r.at[src] for r in refs]
+        return [
+            remote(a, r.at[src], sg_ss.at[level, i], sg_rs.at[level, i], sibling)
+            for i, (a, r) in enumerate(zip(srcs, refs))
+        ]
+
+    def start(copies):
+        for copy in copies:
+            copy.start()
+
+    def arrived(copies):
+        for copy in copies:
+            copy.wait_recv()
+
+    def left(copies):
+        for copy in copies:
+            copy.wait_send()
+
+    start(weights_direct(0, 0) + weights_direct(0, 1))
+
+    @pl.when(has_above)
+    def _():
+        start(token_hop(0, 0, True))
+
+    @pl.when(has_below)
+    def _():
+        start(token_hop(0, 1, True))
+
+    start(token_sibling(z, True))
+    mine = unit_rows(dp)
+    loads = [
+        pltpu.make_async_copy(a, b, load_sem.at[i])
+        for i, (a, b) in enumerate(
+            (
+                (tok_in, tok.at[ex]),
+                (cot_in, cot.at[ex]),
+                (gm_in, gm.at[ex]),
+                (win_in, win.at[:, :, mine]),
+                (wd_in, wd.at[:, mine]),
+            )
+        )
+    ]
+    for load in loads:
+        load.start()
+
+    def token_step(step):
+        @pl.when(z - step - 1 >= 0)
+        def _():
+            arrived(token_hop(step, 0, True))
+            if step + 1 < top:
+                @pl.when(has_above)
+                def _():
+                    start(token_hop(step + 1, 0, False))
+            start(token_sibling(z - step - 1))
+
+        @pl.when(z + step + 1 <= top)
+        def _():
+            arrived(token_hop(step, 1, True))
+            if step + 1 < top:
+                @pl.when(has_below)
+                def _():
+                    start(token_hop(step + 1, 1, False))
+            start(token_sibling(z + step + 1))
+
+    def pass_on(e):
+        arrived(weights_direct(e, 0))
+        start(weights_forward(e, 1))
+        arrived(weights_direct(e, 1))
+        start(weights_forward(e, 0))
+
+    token_step(0)
+    pass_on(0)
+    start(weights_direct(1, 0) + weights_direct(1, 1))
+    for step in range(1, top):
+        token_step(step)
+    for load in loads:
+        load.wait()
+
+    def sibling_arrival(level, carry):
+        arrived(token_sibling(level, True))
+        return carry
+
+    lax.fori_loop(0, levels, sibling_arrival, 0)
+    arrived(weights_forward(0, 0) + weights_forward(0, 1))
+
+    def nt(a, b):
+        return lax.dot_general(a, b, (((1,), (1,)), ((), ())), preferred_element_type=jnp.float32)
+
+    def nn(a, b):
+        return lax.dot_general(a, b, (((1,), (0,)), ((), ())), preferred_element_type=jnp.float32)
+
+    def compute(q, e):
+        both = pl.ds(q * 2, 2)
+        xs = tok[both].reshape(2 * rows, width)
+        cs = cot[both].reshape(2 * rows, width)
+        gmat = gm[both].reshape(2 * rows, gm.shape[2])
+        lane = lax.broadcasted_iota(jnp.int32, gmat.shape, 1)
+        here = lane == ex * win.shape[0] + e
+        g = jnp.sum(jnp.where(here, gmat, 0.0), axis=1, keepdims=True)
+        gate_pre = nt(xs, win[e, 0])
+        up_pre = nt(xs, win[e, 1])
+        gh = nt(cs, wd[e])
+        s = jax.nn.sigmoid(gate_pre)
+        act = gate_pre * s
+        hidden = act * up_pre
+        val = jnp.sum(hidden * gh, axis=1, keepdims=True)
+        out = nn((hidden * g).astype(jnp.bfloat16), wd[e])
+        gh = gh * g
+        grad = nn((gh * up_pre * s * (1.0 + gate_pre * (1.0 - s))).astype(jnp.bfloat16), win[e, 0])
+        grad = grad + nn((gh * act).astype(jnp.bfloat16), win[e, 1])
+        gval = jnp.where(here & (gmat > 0.0), val, 0.0)
+        return (
+            out.reshape(2, rows, width),
+            grad.reshape(2, rows, width),
+            gval.reshape(2, rows, gm.shape[2]),
+        )
+
+    def first_expert(q, carry):
+        out, grad, gval = compute(q, 0)
+        acc[q, :, 0] = out
+        acc[q, :, 1] = grad
+        gacc[q] = gval
+        return carry
+
+    lax.fori_loop(0, levels, first_expert, 0)
+    pass_on(1)
+    arrived(weights_forward(1, 0) + weights_forward(1, 1))
+
+    def level_at(k):
+        tables = ((3, 2, 1, 0), (3, 0, 2, 1), (0, 3, 1, 2), (0, 1, 2, 3))
+        if levels == 2:
+            tables = ((1, 0), (0, 1))
+        q = jnp.int32(0)
+        for i, table in enumerate(tables):
+            for j, level in enumerate(table):
+                q = q + jnp.where((z == i) & (k == j), level, 0)
+        return q
+
+    def to_sibling(q):
+        return [
+            remote(sibs.at[q, h], sibr.at[q, h], sb_ss.at[q, h], sb_rs.at[q, h], sibling) for h in (0, 1)
+        ] + [remote(gsibs.at[q], gsibr.at[q], sb_ss.at[q, 2], sb_rs.at[q, 2], sibling)]
+
+    def chain(q, direction):
+        peer = below if direction else above
+        dst, gdst = (dn, gdn) if direction else (up, gup)
+        rs = dn_rs if direction else up_rs
+        return [
+            remote(snd.at[q, h], dst.at[q, h], ch_ss.at[q, h], rs.at[q, h], peer) for h in (0, 1)
+        ] + [remote(gsnd.at[q], gdst.at[q], ch_ss.at[q, 2], rs.at[q, 2], peer)]
+
+    def produce(k):
+        q = level_at(k)
+        out, grad, gval = compute(q, 1)
+        acc[q, :, 0] += out
+        acc[q, :, 1] += grad
+        gacc[q] += gval
+        other = 1 - c
+        sibs[q] = acc[q, other].astype(sibs.dtype)
+        gsibs[q] = gacc[q, other].T[: gsibs.shape[1]]
+        start(to_sibling(q))
+
+    def take(q, direction):
+        src, gsrc = (dn, gdn) if direction else (up, gup)
+        copies = chain(q, direction)
+        for h in (0, 1):
+            copies[h].wait_recv()
+            acc[q, c, h] += src[q, h].astype(jnp.float32)
+        copies[2].wait_recv()
+        gsnd[q] += gsrc[q]
+
+    def hand_on(q, direction):
+        @pl.when(has_above if direction else has_below)
+        def _():
+            take(q, direction)
+
+        snd[q] = acc[q, c].astype(snd.dtype)
+        start(chain(q, direction))
+
+    def consume(k):
+        q = level_at(k)
+        arrived(to_sibling(q))
+        acc[q, c] += sibr[q].astype(jnp.float32)
+        gsnd[q] = gacc[q, c].T[: gsnd.shape[1]] + gsibr[q]
+
+        @pl.when(q > z)
+        def _():
+            hand_on(q, 0)
+
+        @pl.when(q < z)
+        def _():
+            hand_on(q, 1)
+
+    def turn(k, carry):
+        @pl.when(k < levels)
+        def _():
+            produce(k)
+
+        @pl.when(k > 0)
+        def _():
+            consume(k - 1)
+
+        return carry
+
+    lax.fori_loop(0, levels + 1, turn, 0)
+
+    @pl.when(has_below)
+    def _():
+        take(z, 0)
+
+    @pl.when(has_above)
+    def _():
+        take(z, 1)
+
+    out_ref[...] = acc[z, c, 0].astype(out_ref.dtype)
+    grad_ref[...] = acc[z, c, 1].astype(grad_ref.dtype)
+    gv_ref[...] = gsnd[z]
+
+    for e in (0, 1):
+        for axis in (0, 1):
+            left(weights_direct(e, axis) + weights_forward(e, axis))
+    for step in range(top):
+        @pl.when(has_above & (z - step >= 0))
+        def _():
+            left(token_hop(step, 0, True))
+
+        @pl.when(has_below & (z + step <= top))
+        def _():
+            left(token_hop(step, 1, True))
+
+    def finish(q, carry):
+        left(token_sibling(q, True))
+        left(to_sibling(q))
+
+        @pl.when(q != z)
+        def _():
+            left(chain(q, 0))
+
+        return carry
+
+    lax.fori_loop(0, levels, finish, 0)
+
+
+def fused_body(tokens, expert_ids, router_gates, w_in, w_down, cotangent):
+    rows, width = tokens.shape
+    members = lax.axis_size("expert")
+    exp_local, _, part, _ = w_in.shape
+    experts = exp_local * members
+    units = part * lax.axis_size("dp")
+    levels = members // 2
+    bf16, f32 = jnp.bfloat16, jnp.float32
+    onehot = expert_ids[:, :, None] == jnp.arange(rows, dtype=jnp.int32)
+    gm = jnp.sum(jnp.where(onehot, router_gates[:, :, None], 0.0), axis=1)
+    dma = pltpu.SemaphoreType.DMA
+    vmem = pl.BlockSpec(memory_space=pltpu.VMEM)
+    out, grad, gv = pl.pallas_call(
+        fused_kernel,
+        out_shape=(
+            jax.ShapeDtypeStruct((rows, width), bf16),
+            jax.ShapeDtypeStruct((rows, width), bf16),
+            jax.ShapeDtypeStruct((experts, rows), f32),
+        ),
+        in_specs=[pl.BlockSpec(memory_space=pl.ANY)] * 5,
+        out_specs=(vmem, vmem, vmem),
+        scratch_shapes=[
+            pltpu.VMEM((members, rows, width), bf16),
+            pltpu.VMEM((members, rows, width), bf16),
+            pltpu.VMEM((members, rows, rows), f32),
+            pltpu.VMEM((exp_local, 2, units, width), bf16),
+            pltpu.VMEM((exp_local, units, width), bf16),
+            pltpu.VMEM((levels, 2, 2, rows, width), f32),
+            pltpu.VMEM((levels, 2, rows, rows), f32),
+            pltpu.VMEM((levels, 2, rows, width), bf16),
+            pltpu.VMEM((levels, 2, rows, width), bf16),
+            pltpu.VMEM((levels, experts, rows), f32),
+            pltpu.VMEM((levels, experts, rows), f32),
+            pltpu.VMEM((levels, 2, rows, width), bf16),
+            pltpu.VMEM((levels, experts, rows), f32),
+            pltpu.VMEM((levels, 2, rows, width), bf16),
+            pltpu.VMEM((levels, 2, rows, width), bf16),
+            pltpu.VMEM((levels, experts, rows), f32),
+            pltpu.VMEM((levels, experts, rows), f32),
+            dma((5,)),
+            dma((2, levels - 1, 3)),
+            dma((2, levels - 1, 3)),
+            dma((levels, 3)),
+            dma((levels, 3)),
+            dma((2, 2, 2)),
+            dma((2, 2, 2)),
+            dma((2, 2, 2)),
+            dma((2, 2, 2)),
+            dma((levels, 3)),
+            dma((levels, 3)),
+            dma((levels, 3)),
+            dma((levels, 3)),
+            dma((levels, 3)),
+        ],
+        compiler_params=pltpu.CompilerParams(
+            collective_id=0, has_side_effects=True, vmem_limit_bytes=56 * 2**20
+        ),
+    )(tokens, cotangent, gm, w_in, w_down)
+    gate = jnp.sum(jnp.where(onehot[:, :, :experts], gv.T[:, None, :], 0.0), axis=2)
+    return out, grad, gate
+
+
 def solution(mesh):
     rows = P(("dp", "expert"), None)
     placed = (rows, rows, rows, P("expert", None, "dp", None), P("expert", "dp", None), rows)
+    fits = mesh.shape["dp"] == 4 and mesh.shape["expert"] in (4, 8)
     return jax.shard_map(
-        body, mesh=mesh, in_specs=placed, out_specs=(rows, rows, rows), check_vma=False
+        fused_body if fits else body,
+        mesh=mesh, in_specs=placed, out_specs=(rows, rows, rows), check_vma=False,
     )

time: 306 us -> 129 us (0.42); the launches traced: 300 us -> 128 us
  waiting for transfers between devices: 202 us -> 0 us
  Pallas kernels: 0 us -> 120 us
  matrix products: 40.8 us -> 0 us
  blocking collectives: 28.4 us -> 0 us
  between operations: 14.3 us -> 0.65 us
  other arithmetic: 9.17 us -> 2.8 us
    all_gather x4 -> x0, waiting for transfers between devices: 125 us -> none  [the longest x1 43 us: body(): full_down = lax.all_gather(w_down, 'dp', axis=1, tiled=True)]
    pallas_call x0 -> x1, Pallas kernels: none -> 120 us  [fused_body(): pl.pallas_call(fused_kernel, out_shape=(jax.ShapeDtypeStruct((rows, width...]
    reduce_scatter x3 -> x0, waiting for transfers between devices: 74.7 us -> none  [body(): lax.psum_scatter(v, 'expert', scatter_dimension=0, tiled=True)]
    dot_general x8 -> x0, matrix products: 40.8 us -> none  [dot(): return lax.dot_general(a, b, dims, preferred_element_type=jnp.float32)]
    all_gather x2 -> x0, blocking collectives: 28.4 us -> none  [the longest x1 14.3 us: body(): ids = lax.all_gather(expert_ids, 'expert', axis=0, tiled=True)]
    convert_element_type x1 -> x0, other arithmetic: 8.53 us -> none  [expert_terms(): (gh * up_pre * s * (1.0 + gate_pre * (1.0 - s))).astype(jnp.bfloat16)]
    slice x1 -> x0, local copies, waits for them, and re-layouts: 5.18 us -> none  [expert_terms(): w_pair = full_in[e].reshape(2 * hidden_width, -1)]
    unnamed x22 -> x3, local copies, waits for them, and re-layouts: 0.04 us -> 4.07 us
  transfers between devices with their start and end apart: 7 -> 0, of which waited for: 7 -> 0; matrix products, arithmetic and copies ran while one was open for 14% -> 0% of each run, Pallas kernels for 0% -> 0%
where the time goes in v1:
time: 129 us; the launch traced here: 128 us
  Pallas kernels  120 us (93%)
  local copies, waits for them, and re-layouts  4.07 us (3%)
  other arithmetic  2.8 us (2%)
    pallas_call x1, Pallas kernels, fused_body(): pl.pallas_call(fused_kernel, out_shape=(jax.ShapeDtypeStruct((rows, width...  120 us
    unnamed x3, local copies, waits for them, and re-layouts  4.07 us

profile of v1, /device:TPU:10, one launch (start us, length us, event | category | flops | bytes accessed | tf_op | source)
XLA Modules:
  0.0 127.8 jit_solution(5958786861830999163)
XLA Ops:
  0.6 0.8 select_reduce_fusion
  1.4 0.7 copy.13.gm_in
  2.1 0.7 iota_compare_fusion
  2.9 120.2 %shard_map.85 = (bf16[128,1024]{1,0:T(8,128)(2,1)}, bf16[128,1024]{1,0:T(8,128)(2,1)}, f32[16,128]{1,0:T(8,128)}) custom-call(bf16[128,1024]{1,0:T(8,128)(2,1)} %tok_in.1, bf16[128,1024]{1,0:T(8,128)(2,1)} %cot_in.1, f32[128,128]{1,0:T(8,128)} %copy.13.gm_in, bf16[2,2,176,1024]{3,2,1,0:T(8,128)(2,1)} %win_in.1, bf16[2,176,1024]{2,1,0:T(8,128)(2,1)} %wd_in.1), custom_call_target="tpu_custom_call" | custom-call | tf_op jit(solution)/shard_map/pallas_call | solution.py:394
  123.1 1.3 %select_reduce_fusion.1 = f32[128,6]{0,1:T(8,128)} fusion(pred[128,6,128]{0,2,1:T(8,128)(4,1)S(1)} %iota_compare_fusion, f32[128,16]{0,1:T(8,128)} %bitcast.1), kind=kLoop, calls=%fused_computation.2 | loop fusion | flops 23808 | bytes 23552 | tf_op jit(solution)/shard_map/reduce_sum | solution.py:440
  124.4 1.7 %copy.16 = bf16[128,1024]{1,0:T(8,128)(2,1)} copy(bf16[128,1024]{1,0:T(8,128)(2,1)} %get-tuple-element.12) | data formatting | bytes 524288
  126.1 1.7 %copy.17 = bf16[128,1024]{1,0:T(8,128)(2,1)} copy(bf16[128,1024]{1,0:T(8,128)(2,1)} %get-tuple-element.13) | data formatting | bytes 524288

commit v2 on v1

--- a/solution.py
+++ b/solution.py
@@ -63,7 +63,7 @@
 
 
 def fused_kernel(
-    tok_in, cot_in, gm_in, win_in, wd_in,
+    tok_in, cot_in, ids_in, gates_in, win_in, wd_in,
     out_ref, grad_ref, gv_ref,
     tok, cot, gm, win, wd, acc, gacc, sibs, sibr, gsibs, gsibr, snd, gsnd, up, dn, gup, gdn,
     load_sem, ag_ss, ag_rs, sg_ss, sg_rs, w_ss, w_rs, f_ss, f_rs, sb_ss, sb_rs, ch_ss, up_rs, dn_rs,
@@ -82,6 +82,12 @@
     cut = part // 32 * 16 + 16
     has_above, has_below = z < top, z > 0
 
+    lane = lax.broadcasted_iota(jnp.int32, (rows, rows), 1)
+    choices = ids_in.shape[1]
+    gm[ex] = sum(
+        jnp.where(lane == ids_in[:, k : k + 1], gates_in[:, k : k + 1], 0.0) for k in range(choices)
+    )
+
     barrier = pltpu.get_barrier_semaphore()
     for peer in (sibling, x_peer, y_peer):
         pl.semaphore_signal(barrier, inc=1, device_id=peer, device_id_type=MESH)
@@ -127,7 +133,7 @@
         src = ex + 2 * step if direction else ex - 2 * step
         peer = below if direction else above
         refs = (tok, cot, gm)
-        srcs = (tok_in, cot_in, gm_in) if own else [r.at[src] for r in refs]
+        srcs = (tok_in, cot_in, gm.at[src]) if own else [r.at[src] for r in refs]
         return [
             remote(a, r.at[src], ag_ss.at[direction, step, i], ag_rs.at[direction, step, i], peer)
             for i, (a, r) in enumerate(zip(srcs, refs))
@@ -136,7 +142,7 @@
     def token_sibling(level, own=False):
         refs = (tok, cot, gm)
         src = level * 2 + c
-        srcs = (tok_in, cot_in, gm_in) if own else [r.at[src] for r in refs]
+        srcs = (tok_in, cot_in, gm.at[src]) if own else [r.at[src] for r in refs]
         return [
             remote(a, r.at[src], sg_ss.at[level, i], sg_rs.at[level, i], sibling)
             for i, (a, r) in enumerate(zip(srcs, refs))
@@ -172,7 +178,6 @@
             (
                 (tok_in, tok.at[ex]),
                 (cot_in, cot.at[ex]),
-                (gm_in, gm.at[ex]),
                 (win_in, win.at[:, :, mine]),
                 (wd_in, wd.at[:, mine]),
             )
@@ -227,41 +232,53 @@
     def nn(a, b):
         return lax.dot_general(a, b, (((1,), (0,)), ((), ())), preferred_element_type=jnp.float32)
 
-    def compute(q, e):
+    def compute(q, e, base, size):
         both = pl.ds(q * 2, 2)
+        units = pl.ds(pl.multiple_of(base, 16), size)
         xs = tok[both].reshape(2 * rows, width)
         cs = cot[both].reshape(2 * rows, width)
-        gmat = gm[both].reshape(2 * rows, gm.shape[2])
-        lane = lax.broadcasted_iota(jnp.int32, gmat.shape, 1)
-        here = lane == ex * win.shape[0] + e
+        gmat = gm[both].reshape(2 * rows, rows)
+        here = lax.broadcasted_iota(jnp.int32, gmat.shape, 1) == ex * win.shape[0] + e
         g = jnp.sum(jnp.where(here, gmat, 0.0), axis=1, keepdims=True)
-        gate_pre = nt(xs, win[e, 0])
-        up_pre = nt(xs, win[e, 1])
-        gh = nt(cs, wd[e])
+        gate_pre = nt(xs, win[e, 0, units])
+        up_pre = nt(xs, win[e, 1, units])
+        gh = nt(cs, wd[e, units])
         s = jax.nn.sigmoid(gate_pre)
         act = gate_pre * s
         hidden = act * up_pre
         val = jnp.sum(hidden * gh, axis=1, keepdims=True)
-        out = nn((hidden * g).astype(jnp.bfloat16), wd[e])
+        out = nn((hidden * g).astype(jnp.bfloat16), wd[e, units])
         gh = gh * g
-        grad = nn((gh * up_pre * s * (1.0 + gate_pre * (1.0 - s))).astype(jnp.bfloat16), win[e, 0])
-        grad = grad + nn((gh * act).astype(jnp.bfloat16), win[e, 1])
+        grad_gate = (gh * up_pre * s * (1.0 + gate_pre * (1.0 - s))).astype(jnp.bfloat16)
+        grad = nn(grad_gate, win[e, 0, units])
+        grad = grad + nn((gh * act).astype(jnp.bfloat16), win[e, 1, units])
         gval = jnp.where(here & (gmat > 0.0), val, 0.0)
         return (
             out.reshape(2, rows, width),
             grad.reshape(2, rows, width),
-            gval.reshape(2, rows, gm.shape[2]),
+            gval.reshape(2, rows, rows),
         )
 
+    def add(q, e, base, size):
+        out, grad, gval = compute(q, e, base, size)
+        acc[q, :, 0] += out
+        acc[q, :, 1] += grad
+        gacc[q] += gval
+
     def first_expert(q, carry):
-        out, grad, gval = compute(q, 0)
+        out, grad, gval = compute(q, 0, 0, win.shape[2])
         acc[q, :, 0] = out
         acc[q, :, 1] = grad
         gacc[q] = gval
         return carry
 
+    def near_units(q, carry):
+        add(q, 1, y * 2 * part, 2 * part)
+        return carry
+
     lax.fori_loop(0, levels, first_expert, 0)
     pass_on(1)
+    lax.fori_loop(0, levels, near_units, 0)
     arrived(weights_forward(1, 0) + weights_forward(1, 1))
 
     def level_at(k):
@@ -289,70 +306,84 @@
 
     def produce(k):
         q = level_at(k)
-        out, grad, gval = compute(q, 1)
-        acc[q, :, 0] += out
-        acc[q, :, 1] += grad
-        gacc[q] += gval
+        add(q, 1, (1 - y) * 2 * part, 2 * part)
         other = 1 - c
         sibs[q] = acc[q, other].astype(sibs.dtype)
         gsibs[q] = gacc[q, other].T[: gsibs.shape[1]]
         start(to_sibling(q))
 
-    def take(q, direction):
+    def take(q, direction, h):
         src, gsrc = (dn, gdn) if direction else (up, gup)
         copies = chain(q, direction)
+        copies[h].wait_recv()
+        acc[q, c, h] += src[q, h].astype(jnp.float32)
+        if h:
+            copies[2].wait_recv()
+            gsnd[q] += gsrc[q]
+
+    def hand_on(q, direction, h):
+        @pl.when(has_above if direction else has_below)
+        def _():
+            take(q, direction, h)
+
+        copies = chain(q, direction)
+        snd[q, h] = acc[q, c, h].astype(snd.dtype)
+        copies[h].start()
+        if h:
+            copies[2].start()
+
+    def consume(k, h):
+        q = level_at(k)
+        copies = to_sibling(q)
+        copies[h].wait_recv()
+        acc[q, c, h] += sibr[q, h].astype(jnp.float32)
+        if h:
+            copies[2].wait_recv()
+            gsnd[q] = gacc[q, c].T[: gsnd.shape[1]] + gsibr[q]
+
+        @pl.when(q > z)
+        def _():
+            hand_on(q, 0, h)
+
+        @pl.when(q < z)
+        def _():
+            hand_on(q, 1, h)
+
+    def turn(k, carry):
+        produce(k)
+
+        @pl.when(k == 1)
+        def _():
+            consume(0, 0)
+            consume(0, 1)
+
+        return carry
+
+    lax.fori_loop(0, levels, turn, 0)
+    if levels == 4:
         for h in (0, 1):
-            copies[h].wait_recv()
-            acc[q, c, h] += src[q, h].astype(jnp.float32)
-        copies[2].wait_recv()
-        gsnd[q] += gsrc[q]
-
-    def hand_on(q, direction):
-        @pl.when(has_above if direction else has_below)
-        def _():
-            take(q, direction)
-
-        snd[q] = acc[q, c].astype(snd.dtype)
-        start(chain(q, direction))
-
-    def consume(k):
-        q = level_at(k)
-        arrived(to_sibling(q))
-        acc[q, c] += sibr[q].astype(jnp.float32)
-        gsnd[q] = gacc[q, c].T[: gsnd.shape[1]] + gsibr[q]
-
-        @pl.when(q > z)
-        def _():
-            hand_on(q, 0)
-
-        @pl.when(q < z)
-        def _():
-            hand_on(q, 1)
-
-    def turn(k, carry):
-        @pl.when(k < levels)
-        def _():
-            produce(k)
-
-        @pl.when(k > 0)
-        def _():
-            consume(k - 1)
-
-        return carry
-
-    lax.fori_loop(0, levels + 1, turn, 0)
-
-    @pl.when(has_below)
-    def _():
-        take(z, 0)
-
-    @pl.when(has_above)
-    def _():
-        take(z, 1)
+            consume(1, h)
+            consume(2, h)
+    for h in (0, 1):
+        consume(levels - 1, h)
+
+        @pl.when(has_below)
+        def _():
+            take(z, 0, h)
+
+        @pl.when(has_above)
+        def _():
+            take(z, 1, h)
 
     out_ref[...] = acc[z, c, 0].astype(out_ref.dtype)
     grad_ref[...] = acc[z, c, 1].astype(grad_ref.dtype)
-    gv_ref[...] = gsnd[z]
+    fill = jnp.zeros((rows - gsnd.shape[1], rows), jnp.float32)
+    by_expert = jnp.concatenate([gsnd[z], fill], axis=0).T
+    gate = jnp.zeros((rows, rows), jnp.float32)
+    for k in range(choices):
+        one = jnp.sum(jnp.where(lane == ids_in[:, k : k + 1], by_expert, 0.0), axis=1, keepdims=True)
+        gate = jnp.where(lane == k, one, gate)
+    gv_ref[...] = gate[:, :choices]
 
     for e in (0, 1):
         for axis in (0, 1):
@@ -387,18 +418,17 @@
     units = part * lax.axis_size("dp")
     levels = members // 2
     bf16, f32 = jnp.bfloat16, jnp.float32
-    onehot = expert_ids[:, :, None] == jnp.arange(rows, dtype=jnp.int32)
-    gm = jnp.sum(jnp.where(onehot, router_gates[:, :, None], 0.0), axis=1)
     dma = pltpu.SemaphoreType.DMA
     vmem = pl.BlockSpec(memory_space=pltpu.VMEM)
-    out, grad, gv = pl.pallas_call(
+    hbm = pl.BlockSpec(memory_space=pl.ANY)
+    return pl.pallas_call(
         fused_kernel,
         out_shape=(
             jax.ShapeDtypeStruct((rows, width), bf16),
             jax.ShapeDtypeStruct((rows, width), bf16),
-            jax.ShapeDtypeStruct((experts, rows), f32),
+            jax.ShapeDtypeStruct(router_gates.shape, f32),
         ),
-        in_specs=[pl.BlockSpec(memory_space=pl.ANY)] * 5,
+        in_specs=[hbm, hbm, vmem, vmem, hbm, hbm],
         out_specs=(vmem, vmem, vmem),
         scratch_shapes=[
             pltpu.VMEM((members, rows, width), bf16),
@@ -418,7 +448,7 @@
             pltpu.VMEM((levels, 2, rows, width), bf16),
             pltpu.VMEM((levels, experts, rows), f32),
             pltpu.VMEM((levels, experts, rows), f32),
-            dma((5,)),
+            dma((4,)),
             dma((2, levels - 1, 3)),
             dma((2, levels - 1, 3)),
             dma((levels, 3)),
@@ -436,9 +466,7 @@
         compiler_params=pltpu.CompilerParams(
             collective_id=0, has_side_effects=True, vmem_limit_bytes=56 * 2**20
         ),
-    )(tokens, cotangent, gm, w_in, w_down)
-    gate = jnp.sum(jnp.where(onehot[:, :, :experts], gv.T[:, None, :], 0.0), axis=2)
-    return out, grad, gate
+    )(tokens, cotangent, expert_ids, router_gates, w_in, w_down)
 
 
 def solution(mesh):

time: 129 us -> 130 us (level)
  local copies, waits for them, and re-layouts: 4.07 us -> 7.69 us
  other arithmetic: 2.8 us -> 0 us
    unnamed x3 -> x4, local copies, waits for them, and re-layouts: 4.07 us -> 6.18 us
    reduce_sum x2 -> x0, other arithmetic: 2.06 us -> none  [the longest x1 1.31 us: fused_body(): jnp.sum(jnp.where(onehot[:, :, :experts], gv.T[:, None, :], 0.0), axis=2)]
    pallas_call x0 -> x1, local copies, waits for them, and re-layouts: none -> 1.51 us  [fused_body(): pl.pallas_call(fused_kernel, out_shape=(jax.ShapeDtypeStruct((rows, width...]
where the time goes in v2:
time: 130 us
  Pallas kernels  121 us (93%)
  local copies, waits for them, and re-layouts  7.69 us (6%)
    pallas_call x1, Pallas kernels, fused_body(): pl.pallas_call(fused_kernel, out_shape=(jax.ShapeDtypeStruct((rows, width...  121 us
    unnamed x4, local copies, waits for them, and re-layouts  6.18 us

profile of v2, /device:TPU:10, one launch (start us, length us, event | category | flops | bytes accessed | tf_op | source)
XLA Modules:
  0.0 129.5 jit_solution(15577076352947771582)
XLA Ops:
  0.6 1.4 %copy.9.ids_in = s32[128,6]{1,0:T(8,128)} copy(s32[128,6]{0,1:T(8,128)} %param.7) | data formatting | bytes 6144 | tf_op args[1]
  2.1 1.4 %copy.10.gates_in = f32[128,6]{1,0:T(8,128)} copy(f32[128,6]{0,1:T(8,128)} %param.8) | data formatting | bytes 6144 | tf_op args[2]
  3.5 121.2 %shard_map.85 = (bf16[128,1024]{1,0:T(8,128)(2,1)}, bf16[128,1024]{1,0:T(8,128)(2,1)}, f32[128,6]{1,0:T(8,128)}) custom-call(bf16[128,1024]{1,0:T(8,128)(2,1)} %tok_in.1, bf16[128,1024]{1,0:T(8,128)(2,1)} %cot_in.1, s32[128,6]{1,0:T(8,128)} %copy.9.ids_in, f32[128,6]{1,0:T(8,128)} %copy.10.gates_in, bf16[2,2,176,1024]{3,2,1,0:T(8,128)(2,1)} %win_in.1, ...), custom_call_target="tpu_custom_call" | custom-call | tf_op jit(solution)/shard_map/pallas_call | solution.py:424
  124.7 1.5 %copy.11 = f32[128,6]{0,1:T(8,128)} copy(f32[128,6]{1,0:T(8,128)} %get-tuple-element.5) | data formatting | bytes 6144 | tf_op jit(solution)/shard_map/pallas_call | solution.py:424
  126.2 1.7 %copy.14 = bf16[128,1024]{1,0:T(8,128)(2,1)} copy(bf16[128,1024]{1,0:T(8,128)(2,1)} %get-tuple-element.9) | data formatting | bytes 524288
  127.9 1.7 %copy.15 = bf16[128,1024]{1,0:T(8,128)(2,1)} copy(bf16[128,1024]{1,0:T(8,128)(2,1)} %get-tuple-element.10) | data formatting | bytes 524288

commit v3 on v2

--- a/solution.py
+++ b/solution.py
@@ -65,7 +65,7 @@
 def fused_kernel(
     tok_in, cot_in, ids_in, gates_in, win_in, wd_in,
     out_ref, grad_ref, gv_ref,
-    tok, cot, gm, win, wd, acc, gacc, sibs, sibr, gsibs, gsibr, snd, gsnd, up, dn, gup, gdn,
+    tok, cot, gm, win, wd, acc, gacc, pick, xrow, crow, orow, drow, vrow, sibs, sibr, gsibs, gsibr, snd, gsnd, up, dn, gup, gdn,
     load_sem, ag_ss, ag_rs, sg_ss, sg_rs, w_ss, w_rs, f_ss, f_rs, sb_ss, sb_rs, ch_ss, up_rs, dn_rs,
 ):
     dp, ex = lax.axis_index("dp"), lax.axis_index("expert")
@@ -82,10 +82,10 @@
     cut = part // 32 * 16 + 16
     has_above, has_below = z < top, z > 0
 
-    lane = lax.broadcasted_iota(jnp.int32, (rows, rows), 1)
-    choices = ids_in.shape[1]
+    experts, choices = gm.shape[1], ids_in.shape[0]
+    expert_row = lax.broadcasted_iota(jnp.int32, (experts, rows), 0)
     gm[ex] = sum(
-        jnp.where(lane == ids_in[:, k : k + 1], gates_in[:, k : k + 1], 0.0) for k in range(choices)
+        jnp.where(expert_row == ids_in[k : k + 1], gates_in[k : k + 1], 0.0) for k in range(choices)
     )
 
     barrier = pltpu.get_barrier_semaphore()
@@ -224,22 +224,51 @@
         return carry
 
     lax.fori_loop(0, levels, sibling_arrival, 0)
-    arrived(weights_forward(0, 0) + weights_forward(0, 1))
-
     def nt(a, b):
         return lax.dot_general(a, b, (((1,), (1,)), ((), ())), preferred_element_type=jnp.float32)
 
     def nn(a, b):
         return lax.dot_general(a, b, (((1,), (0,)), ((), ())), preferred_element_type=jnp.float32)
 
-    def compute(q, e, base, size):
+    def tn(a, b):
+        return lax.dot_general(a, b, (((0,), (0,)), ((), ())), preferred_element_type=jnp.float32)
+
+    slots = pick.shape[2]
+    span = (2 * rows, 2 * rows)
+    earlier = lax.broadcasted_iota(jnp.int32, span, 0) < lax.broadcasted_iota(jnp.int32, span, 1)
+    earlier = jnp.where(earlier, 1.0, 0.0).astype(jnp.bfloat16)
+    slot = lax.broadcasted_iota(jnp.int32, (slots, 2 * rows), 0).astype(jnp.float32)
+
+    def gate_line(q, e):
+        own = expert_row == ex * win.shape[0] + e
+        halves = [jnp.sum(jnp.where(own, gm[q * 2 + d], 0.0), axis=0, keepdims=True) for d in (0, 1)]
+        return jnp.concatenate(halves, axis=1)
+
+    def gather(q, carry):
         both = pl.ds(q * 2, 2)
-        units = pl.ds(pl.multiple_of(base, 16), size)
         xs = tok[both].reshape(2 * rows, width)
         cs = cot[both].reshape(2 * rows, width)
-        gmat = gm[both].reshape(2 * rows, rows)
-        here = lax.broadcasted_iota(jnp.int32, gmat.shape, 1) == ex * win.shape[0] + e
-        g = jnp.sum(jnp.where(here, gmat, 0.0), axis=1, keepdims=True)
+        for e in (0, 1):
+            chosen = jnp.where(gate_line(q, e) > 0.0, 1.0, 0.0)
+            rank = nn(jnp.broadcast_to(chosen, (16, 2 * rows)).astype(jnp.bfloat16), earlier)[:1]
+            place = jnp.where((slot == rank) & (chosen > 0.0), 1.0, 0.0).astype(jnp.bfloat16)
+            pick[e, q] = place
+            xrow[e, q] = nn(place, xs).astype(jnp.bfloat16)
+            crow[e, q] = nn(place, cs).astype(jnp.bfloat16)
+        return carry
+
+    def gate_rows(e):
+        parts = [
+            jnp.sum(jnp.where(pick[e, q].astype(jnp.float32) > 0.0, gate_line(q, e), 0.0), axis=1, keepdims=True)
+            for q in range(levels)
+        ]
+        return jnp.concatenate(parts, axis=0)
+
+    def compute(e, base, size, first):
+        units = pl.ds(pl.multiple_of(base, 16), size)
+        xs = xrow[e].reshape(levels * slots, width)
+        cs = crow[e].reshape(levels * slots, width)
+        g = gate_rows(e)
         gate_pre = nt(xs, win[e, 0, units])
         up_pre = nt(xs, win[e, 1, units])
         gh = nt(cs, wd[e, units])
@@ -252,34 +281,43 @@
         grad_gate = (gh * up_pre * s * (1.0 + gate_pre * (1.0 - s))).astype(jnp.bfloat16)
         grad = nn(grad_gate, win[e, 0, units])
         grad = grad + nn((gh * act).astype(jnp.bfloat16), win[e, 1, units])
-        gval = jnp.where(here & (gmat > 0.0), val, 0.0)
-        return (
-            out.reshape(2, rows, width),
-            grad.reshape(2, rows, width),
-            gval.reshape(2, rows, rows),
-        )
-
-    def add(q, e, base, size):
-        out, grad, gval = compute(q, e, base, size)
-        acc[q, :, 0] += out
-        acc[q, :, 1] += grad
-        gacc[q] += gval
-
-    def first_expert(q, carry):
-        out, grad, gval = compute(q, 0, 0, win.shape[2])
-        acc[q, :, 0] = out
-        acc[q, :, 1] = grad
-        gacc[q] = gval
+        for ref, new in ((orow, out), (drow, grad), (vrow, jnp.broadcast_to(val, (levels * slots, rows)))):
+            new = new.reshape(ref.shape)
+            if first:
+                ref[...] = new
+            else:
+                ref[...] += new
+
+    def scatter(q, e, first):
+        place = pick[e, q]
+        out = tn(place, orow[q].astype(jnp.bfloat16)).reshape(2, rows, width)
+        grad = tn(place, drow[q].astype(jnp.bfloat16)).reshape(2, rows, width)
+        line = jnp.where(place.astype(jnp.float32) > 0.0, vrow[q][:, :1], 0.0)
+        line = jnp.sum(line, axis=0, keepdims=True)
+        own = expert_row == ex * win.shape[0] + e
+        for d in (0, 1):
+            gval = jnp.where(own, line[:, d * rows : (d + 1) * rows], 0.0)
+            if first:
+                acc[q, d, 0] = out[d]
+                acc[q, d, 1] = grad[d]
+                gacc[q, d] = gval
+            else:
+                acc[q, d, 0] += out[d]
+                acc[q, d, 1] += grad[d]
+                gacc[q, d] += gval
+
+    def first_scatter(q, carry):
+        scatter(q, 0, True)
         return carry
 
-    def near_units(q, carry):
-        add(q, 1, y * 2 * part, 2 * part)
-        return carry
-
-    lax.fori_loop(0, levels, first_expert, 0)
+    lax.fori_loop(0, levels, gather, 0)
+    arrived(weights_forward(0, 0) + weights_forward(0, 1))
+    compute(0, 0, win.shape[2], True)
+    lax.fori_loop(0, levels, first_scatter, 0)
     pass_on(1)
-    lax.fori_loop(0, levels, near_units, 0)
+    compute(1, y * 2 * part, 2 * part, True)
     arrived(weights_forward(1, 0) + weights_forward(1, 1))
+    compute(1, (1 - y) * 2 * part, 2 * part, False)
 
     def level_at(k):
         tables = ((3, 2, 1, 0), (3, 0, 2, 1), (0, 3, 1, 2), (0, 1, 2, 3))
@@ -306,10 +344,10 @@
 
     def produce(k):
         q = level_at(k)
-        add(q, 1, (1 - y) * 2 * part, 2 * part)
+        scatter(q, 1, False)
         other = 1 - c
         sibs[q] = acc[q, other].astype(sibs.dtype)
-        gsibs[q] = gacc[q, other].T[: gsibs.shape[1]]
+        gsibs[q] = gacc[q, other]
         start(to_sibling(q))
 
     def take(q, direction, h):
@@ -339,7 +377,7 @@
         acc[q, c, h] += sibr[q, h].astype(jnp.float32)
         if h:
             copies[2].wait_recv()
-            gsnd[q] = gacc[q, c].T[: gsnd.shape[1]] + gsibr[q]
+            gsnd[q] = gacc[q, c] + gsibr[q]
 
         @pl.when(q > z)
         def _():
@@ -377,13 +415,9 @@
 
     out_ref[...] = acc[z, c, 0].astype(out_ref.dtype)
     grad_ref[...] = acc[z, c, 1].astype(grad_ref.dtype)
-    fill = jnp.zeros((rows - gsnd.shape[1], rows), jnp.float32)
-    by_expert = jnp.concatenate([gsnd[z], fill], axis=0).T
-    gate = jnp.zeros((rows, rows), jnp.float32)
     for k in range(choices):
-        one = jnp.sum(jnp.where(lane == ids_in[:, k : k + 1], by_expert, 0.0), axis=1, keepdims=True)
-        gate = jnp.where(lane == k, one, gate)
-    gv_ref[...] = gate[:, :choices]
+        named = expert_row == ids_in[k : k + 1]
+        gv_ref[k : k + 1] = jnp.sum(jnp.where(named, gsnd[z], 0.0), axis=0, keepdims=True)
 
     for e in (0, 1):
         for axis in (0, 1):
@@ -417,27 +451,36 @@
     experts = exp_local * members
     units = part * lax.axis_size("dp")
     levels = members // 2
+    choices = expert_ids.shape[1]
+    capacity = rows * choices // experts + 1
+    slots = -(-2 * capacity // 16) * 16
     bf16, f32 = jnp.bfloat16, jnp.float32
     dma = pltpu.SemaphoreType.DMA
     vmem = pl.BlockSpec(memory_space=pltpu.VMEM)
     hbm = pl.BlockSpec(memory_space=pl.ANY)
-    return pl.pallas_call(
+    out, grad, gate = pl.pallas_call(
         fused_kernel,
         out_shape=(
             jax.ShapeDtypeStruct((rows, width), bf16),
             jax.ShapeDtypeStruct((rows, width), bf16),
-            jax.ShapeDtypeStruct(router_gates.shape, f32),
+            jax.ShapeDtypeStruct((choices, rows), f32),
         ),
         in_specs=[hbm, hbm, vmem, vmem, hbm, hbm],
         out_specs=(vmem, vmem, vmem),
         scratch_shapes=[
             pltpu.VMEM((members, rows, width), bf16),
             pltpu.VMEM((members, rows, width), bf16),
-            pltpu.VMEM((members, rows, rows), f32),
+            pltpu.VMEM((members, experts, rows), f32),
             pltpu.VMEM((exp_local, 2, units, width), bf16),
             pltpu.VMEM((exp_local, units, width), bf16),
             pltpu.VMEM((levels, 2, 2, rows, width), f32),
-            pltpu.VMEM((levels, 2, rows, rows), f32),
+            pltpu.VMEM((levels, 2, experts, rows), f32),
+            pltpu.VMEM((exp_local, levels, slots, 2 * rows), bf16),
+            pltpu.VMEM((exp_local, levels, slots, width), bf16),
+            pltpu.VMEM((exp_local, levels, slots, width), bf16),
+            pltpu.VMEM((levels, slots, width), f32),
+            pltpu.VMEM((levels, slots, width), f32),
+            pltpu.VMEM((levels, slots, rows), f32),
             pltpu.VMEM((levels, 2, rows, width), bf16),
             pltpu.VMEM((levels, 2, rows, width), bf16),
             pltpu.VMEM((levels, experts, rows), f32),
@@ -466,7 +509,8 @@
         compiler_params=pltpu.CompilerParams(
             collective_id=0, has_side_effects=True, vmem_limit_bytes=56 * 2**20
         ),
-    )(tokens, cotangent, expert_ids, router_gates, w_in, w_down)
+    )(tokens, cotangent, expert_ids.T, router_gates.T, w_in, w_down)
+    return out, grad, gate.T
 
 
 def solution(mesh):

time: 130 us -> 129 us (level)
  local copies, waits for them, and re-layouts: 7.69 us -> 4.6 us
  Pallas kernels: 121 us -> 123 us
    pallas_call x1, Pallas kernels: 121 us -> 123 us  [fused_body(): pl.pallas_call(fused_kernel, out_shape=(jax.ShapeDtypeStruct((rows, width...]
    unnamed x4 -> x3, local copies, waits for them, and re-layouts: 6.18 us -> 4.6 us
    pallas_call x1 -> x0, local copies, waits for them, and re-layouts: 1.51 us -> none  [fused_body(): pl.pallas_call(fused_kernel, out_shape=(jax.ShapeDtypeStruct((rows, width...]
where the time goes in v3:
time: 129 us; the launch traced here: 128 us
  Pallas kernels  123 us (95%)
  local copies, waits for them, and re-layouts  4.6 us (4%)
    pallas_call x1, Pallas kernels, fused_body(): pl.pallas_call(fused_kernel, out_shape=(jax.ShapeDtypeStruct((rows, width...  123 us
    unnamed x3, local copies, waits for them, and re-layouts  4.6 us

profile of v3, /device:TPU:10, one launch (start us, length us, event | category | flops | bytes accessed | tf_op | source)
XLA Modules:
  0.0 128.3 jit_solution(14659859847416930979)
XLA Ops:
  0.6 123.0 %shard_map.85 = (bf16[128,1024]{1,0:T(8,128)(2,1)}, bf16[128,1024]{1,0:T(8,128)(2,1)}, f32[6,128]{1,0:T(8,128)}) custom-call(bf16[128,1024]{1,0:T(8,128)(2,1)} %tok_in.1, bf16[128,1024]{1,0:T(8,128)(2,1)} %cot_in.1, s32[6,128]{1,0:T(8,128)} %bitcast.3, f32[6,128]{1,0:T(8,128)} %bitcast.4, bf16[2,2,176,1024]{3,2,1,0:T(8,128)(2,1)} %win_in.1, ...), custom_call_target="tpu_custom_call" | custom-call | tf_op jit(solution)/shard_map/pallas_call | solution.py:461
  123.7 1.7 %copy.12 = bf16[128,1024]{1,0:T(8,128)(2,1)} copy(bf16[128,1024]{1,0:T(8,128)(2,1)} %get-tuple-element.12) | data formatting | bytes 524288
  125.4 1.7 %copy.13 = bf16[128,1024]{1,0:T(8,128)(2,1)} copy(bf16[128,1024]{1,0:T(8,128)(2,1)} %get-tuple-element.13) | data formatting | bytes 524288
  127.0 1.3 copy.14

commit v4 on v3

--- a/solution.py
+++ b/solution.py
@@ -212,8 +212,8 @@
         start(weights_forward(e, 0))
 
     token_step(0)
+    start(weights_direct(1, 0) + weights_direct(1, 1))
     pass_on(0)
-    start(weights_direct(1, 0) + weights_direct(1, 1))
     for step in range(1, top):
         token_step(step)
     for load in loads:
@@ -311,13 +311,14 @@
         return carry
 
     lax.fori_loop(0, levels, gather, 0)
+    pass_on(1)
     arrived(weights_forward(0, 0) + weights_forward(0, 1))
     compute(0, 0, win.shape[2], True)
     lax.fori_loop(0, levels, first_scatter, 0)
-    pass_on(1)
     compute(1, y * 2 * part, 2 * part, True)
+    compute(1, dp_y * part, part, False)
     arrived(weights_forward(1, 0) + weights_forward(1, 1))
-    compute(1, (1 - y) * 2 * part, 2 * part, False)
+    compute(1, ((1 - y) * 2 + 1 - x) * part, part, False)
 
     def level_at(k):
         tables = ((3, 2, 1, 0), (3, 0, 2, 1), (0, 3, 1, 2), (0, 1, 2, 3))

time: 129 us -> 127 us (0.984)
  Pallas kernels: 123 us -> 120 us
    pallas_call x1, Pallas kernels: 123 us -> 120 us  [fused_body(): pl.pallas_call(fused_kernel, out_shape=(jax.ShapeDtypeStruct((rows, width...]
where the time goes in v4:
time: 127 us; the launch traced here: 125 us
  Pallas kernels  120 us (94%)
  local copies, waits for them, and re-layouts  4.6 us (4%)
    pallas_call x1, Pallas kernels, fused_body(): pl.pallas_call(fused_kernel, out_shape=(jax.ShapeDtypeStruct((rows, width...  120 us
    unnamed x3, local copies, waits for them, and re-layouts  4.6 us

profile of v4, /device:TPU:10, one launch (start us, length us, event | category | flops | bytes accessed | tf_op | source)
XLA Modules:
  0.0 125.2 jit_solution(17660769788280661473)
XLA Ops:
  0.6 119.9 %shard_map.85 = (bf16[128,1024]{1,0:T(8,128)(2,1)}, bf16[128,1024]{1,0:T(8,128)(2,1)}, f32[6,128]{1,0:T(8,128)}) custom-call(bf16[128,1024]{1,0:T(8,128)(2,1)} %tok_in.1, bf16[128,1024]{1,0:T(8,128)(2,1)} %cot_in.1, s32[6,128]{1,0:T(8,128)} %bitcast.3, f32[6,128]{1,0:T(8,128)} %bitcast.4, bf16[2,2,176,1024]{3,2,1,0:T(8,128)(2,1)} %win_in.1, ...), custom_call_target="tpu_custom_call" | custom-call | tf_op jit(solution)/shard_map/pallas_call | solution.py:462
  120.6 1.7 %copy.12 = bf16[128,1024]{1,0:T(8,128)(2,1)} copy(bf16[128,1024]{1,0:T(8,128)(2,1)} %get-tuple-element.12) | data formatting | bytes 524288
  122.2 1.7 %copy.13 = bf16[128,1024]{1,0:T(8,128)(2,1)} copy(bf16[128,1024]{1,0:T(8,128)(2,1)} %get-tuple-element.13) | data formatting | bytes 524288
  123.9 1.3 %copy.14 = f32[128,6]{0,1:T(8,128)} copy(f32[128,6]{0,1:T(8,128)} %bitcast.5) | data formatting | bytes 6144

commit v5 on v4

--- a/solution.py
+++ b/solution.py
@@ -462,8 +462,8 @@
     out, grad, gate = pl.pallas_call(
         fused_kernel,
         out_shape=(
-            jax.ShapeDtypeStruct((rows, width), bf16),
-            jax.ShapeDtypeStruct((rows, width), bf16),
+            jax.ShapeDtypeStruct((rows, width), f32),
+            jax.ShapeDtypeStruct((rows, width), f32),
             jax.ShapeDtypeStruct((choices, rows), f32),
         ),
         in_specs=[hbm, hbm, vmem, vmem, hbm, hbm],
@@ -511,7 +511,7 @@
             collective_id=0, has_side_effects=True, vmem_limit_bytes=56 * 2**20
         ),
     )(tokens, cotangent, expert_ids.T, router_gates.T, w_in, w_down)
-    return out, grad, gate.T
+    return out.astype(bf16), grad.astype(bf16), gate.T
 
 
 def solution(mesh):

time: 127 us -> 126 us (level)
  local copies, waits for them, and re-layouts: 4.6 us -> 0.6 us
  other arithmetic: 0 us -> 3.56 us
    unnamed x3, local copies, waits for them, and re-layouts: 4.6 us -> 0.6 us
    convert_element_type x0 -> x2, other arithmetic: none -> 3.56 us  [fused_body(): return (out.astype(bf16), grad.astype(bf16), gate.T)]
where the time goes in v5:
time: 126 us; the launch traced here: 125 us
  Pallas kernels  120 us (95%)
  other arithmetic  3.56 us (3%)
    pallas_call x1, Pallas kernels, fused_body(): pl.pallas_call(fused_kernel, out_shape=(jax.ShapeDtypeStruct((rows, width...  120 us
    convert_element_type x2, other arithmetic, fused_body(): return (out.astype(bf16), grad.astype(bf16), gate.T)  3.56 us

profile of v5, /device:TPU:10, one launch (start us, length us, event | category | flops | bytes accessed | tf_op | source)
XLA Modules:
  0.0 124.9 jit_solution(7362845856517150088)
XLA Ops:
  0.6 120.1 %shard_map.85 = (f32[128,1024]{1,0:T(8,128)}, f32[128,1024]{1,0:T(8,128)}, f32[6,128]{1,0:T(8,128)}) custom-call(bf16[128,1024]{1,0:T(8,128)(2,1)} %tok_in.1, bf16[128,1024]{1,0:T(8,128)(2,1)} %cot_in.1, s32[6,128]{1,0:T(8,128)} %bitcast.3, f32[6,128]{1,0:T(8,128)} %bitcast.4, bf16[2,2,176,1024]{3,2,1,0:T(8,128)(2,1)} %win_in.1, bf16[2,176,1024]{2,1,0:T(8,128)(2,1)} %wd_in.1), custom_call_target="tpu_custom_call" | custom-call | tf_op jit(solution)/shard_map/pallas_call | solution.py:462
  120.8 0.0 copy-start
  120.8 1.8 %convert_element_type.6 = bf16[128,1024]{1,0:T(8,128)(2,1)} convert(f32[128,1024]{1,0:T(8,128)} %get-tuple-element.6) | non-fusion elementwise | flops 131072 | bytes 786432 | tf_op jit(solution)/shard_map/convert_element_type | solution.py:514
  122.5 1.8 %convert_element_type.7 = bf16[128,1024]{1,0:T(8,128)(2,1)} convert(f32[128,1024]{1,0:T(8,128)} %get-tuple-element.7) | non-fusion elementwise | flops 131072 | bytes 786432 | tf_op jit(solution)/shard_map/convert_element_type | solution.py:514
  124.3 0.0 copy-done
  124.3 0.6 copy.10
Async XLA Ops:
  120.8 3.6 %copy-start = (f32[6,128]{1,0:T(8,128)S(1)}, f32[6,128]{1,0:T(8,128)}, u32[]{:S(2)}) copy-start(f32[6,128]{1,0:T(8,128)} %get-tuple-element.8) | copy-start | bytes 9220

commit v6 on v4

--- a/solution.py
+++ b/solution.py
@@ -206,10 +206,10 @@
             start(token_sibling(z + step + 1))
 
     def pass_on(e):
-        arrived(weights_direct(e, 0))
-        start(weights_forward(e, 1))
-        arrived(weights_direct(e, 1))
-        start(weights_forward(e, 0))
+        for i in (0, 1):
+            for axis in (0, 1):
+                weights_direct(e, axis)[i].wait_recv()
+                weights_forward(e, 1 - axis)[i].start()
 
     token_step(0)
     start(weights_direct(1, 0) + weights_direct(1, 1))

time: 127 us -> 127 us (level)
  no operation moved by 1% of the time
where the time goes in v6:
time: 127 us; the launch traced here: 125 us
  Pallas kernels  120 us (94%)
  local copies, waits for them, and re-layouts  4.6 us (4%)
    pallas_call x1, Pallas kernels, fused_body(): pl.pallas_call(fused_kernel, out_shape=(jax.ShapeDtypeStruct((rows, width...  120 us
    unnamed x3, local copies, waits for them, and re-layouts  4.6 us

profile of v6, /device:TPU:10, one launch (start us, length us, event | category | flops | bytes accessed | tf_op | source)
XLA Modules:
  0.0 125.2 jit_solution(4543229300945782528)
XLA Ops:
  0.6 119.9 %shard_map.85 = (bf16[128,1024]{1,0:T(8,128)(2,1)}, bf16[128,1024]{1,0:T(8,128)(2,1)}, f32[6,128]{1,0:T(8,128)}) custom-call(bf16[128,1024]{1,0:T(8,128)(2,1)} %tok_in.1, bf16[128,1024]{1,0:T(8,128)(2,1)} %cot_in.1, s32[6,128]{1,0:T(8,128)} %bitcast.3, f32[6,128]{1,0:T(8,128)} %bitcast.4, bf16[2,2,176,1024]{3,2,1,0:T(8,128)(2,1)} %win_in.1, ...), custom_call_target="tpu_custom_call" | custom-call | tf_op jit(solution)/shard_map/pallas_call | solution.py:462
  120.6 1.7 %copy.12 = bf16[128,1024]{1,0:T(8,128)(2,1)} copy(bf16[128,1024]{1,0:T(8,128)(2,1)} %get-tuple-element.12) | data formatting | bytes 524288
  122.2 1.7 %copy.13 = bf16[128,1024]{1,0:T(8,128)(2,1)} copy(bf16[128,1024]{1,0:T(8,128)(2,1)} %get-tuple-element.13) | data formatting | bytes 524288
  123.9 1.3 %copy.14 = f32[128,6]{0,1:T(8,128)} copy(f32[128,6]{0,1:T(8,128)} %bitcast.5) | data formatting | bytes 6144
